TPU v7x, 32 devices: a whole 2x2x4 slice. The times are simulated.
32 devices in a mesh: dp: 2 (over x), tensor: 16 (over z, y, core).
Axes of the slice: x: 2, y: 2, z: 4, core: 2. Of those that a mesh axis runs over, the one named last changes fastest.
Arguments:
- grad_out: bfloat16 [512, 16384], P('tensor', 'dp'), may hold values from -6 to 6
- hidden: bfloat16 [512, 26624], P('dp', 'tensor'), may hold values from -0.25 to 0.25
- down_weight: bfloat16 [26624, 16384], P('tensor', 'dp'), may hold values from -0.046875 to 0.046875
Outputs:
- grad_hidden: bfloat16 [512, 26624], P('dp', 'tensor')
- grad_weight: bfloat16 [26624, 16384], P('tensor', 'dp')
All inputs are finite; a program needn't handle non-finite values.
Results may differ from a plain program's by a relative error of at most 0.0052.
Values may be sent and summed in bfloat16 or wider, within the bound.
A program may use at most 192 MiB of HBM per device.

v0:
```python
import jax
import jax.numpy as jnp
from jax import lax
from jax.sharding import PartitionSpec as P


def local(grad_out, hidden, down_weight):
    hidden_all = lax.all_gather(hidden, "dp", axis=0, tiled=True)
    grad_all = lax.all_gather(grad_out, "tensor", axis=0, tiled=True)
    weight_grad = lax.dot_general(
        hidden_all, grad_all, (((0,), (0,)), ((), ())), preferred_element_type=jnp.float32
    )
    grad_hidden = lax.psum_scatter(
        lax.dot_general(
            grad_all, down_weight, (((1,), (1,)), ((), ())), preferred_element_type=jnp.float32
        ).astype(jnp.bfloat16),
        "dp",
        scatter_dimension=0,
        tiled=True,
    )
    return (grad_hidden, weight_grad.astype(jnp.bfloat16))


def solution(mesh):
    placed = (P("tensor", "dp"), P("dp", "tensor"), P("tensor", "dp"))
    return jax.shard_map(
        local,
        mesh=mesh,
        in_specs=placed,
        out_specs=(P("dp", "tensor"), P("tensor", "dp")),
        check_vma=False,
    )
```

profile of v0, /device:TPU:8, one launch (start us, length us, event | category | flops | bytes accessed | tf_op | source)
XLA Modules:
  0.0 151.7 jit_solution(6932774043005715514)
XLA Ops:
  7.2 0.0 all-gather.3.cloned.1.call-start
  7.2 0.7 all-gather.3.cloned.1.call-update
  7.9 0.0 all-gather.5.cloned.1.call-start
  7.9 0.7 all-gather.5.cloned.1.call-update
  8.6 0.0 reduce-scatter.2.cloned.1.call-start
  8.7 77.0 %all-gather.3.cloned.1.call-done = bf16[512,8192]{1,0:T(8,128)(2,1)} async-done(((bf16[32,8192]{1,0:T(8,128)(2,1)}), bf16[512,8192]{1,0:T(8,128)(2,1)}) %all-gather.3.cloned.1.call-update) | async-done | bytes 8388624 | tf_op jit(solution)/shard_map/all_gather | solution.py:9
  85.7 22.1 %convolution_convert_fusion.1 = bf16[512,1664]{1,0:T(8,128)(2,1)} fusion(bf16[512,8192]{1,0:T(8,128)(2,1)} %all-gather.3.cloned.1.call-done, bf16[1664,8192]{1,0:T(8,128)(2,1)} %param.5), kind=kOutput, calls=%fused_computation.1 | convolution fusion | flops 13959495680 | bytes 37355520 | tf_op jit(solution)/shard_map/dot_general | solution.py:14
  107.8 0.0 reduce-scatter.2.cloned.1.call-update
  107.8 7.0 %all-gather.5.cloned.1.call-done = bf16[512,1664]{1,0:T(8,128)(2,1)} async-done(((bf16[256,1664]{1,0:T(8,128)(2,1)}), bf16[512,1664]{1,0:T(8,128)(2,1)}) %all-gather.5.cloned.1.call-update) | async-done | bytes 1703952 | tf_op jit(solution)/shard_map/all_gather | solution.py:8
  114.8 21.0 %convolution_convert_fusion = bf16[1664,8192]{1,0:T(8,128)(2,1)} fusion(bf16[512,1664]{1,0:T(8,128)(2,1)} %all-gather.5.cloned.1.call-done, bf16[512,8192]{1,0:T(8,128)(2,1)} %all-gather.3.cloned.1.call-done), kind=kOutput, calls=%fused_computation | convolution fusion | flops 13972275200 | bytes 37355520 | tf_op jit(solution)/shard_map/dot_general | solution.py:10
  135.8 9.3 %reduce-scatter.2.cloned.1.call-done = bf16[256,1664]{1,0:T(8,128)(2,1)} async-done(((bf16[512,1664]{1,0:T(8,128)(2,1)}), bf16[256,1664]{1,0:T(8,128)(2,1)}) %reduce-scatter.2.cloned.1.call-update) | async-done | bytes 851984 | tf_op jit(solution)/shard_map/reduce_scatter | solution.py:13
Async XLA Ops:
  7.2 78.5 %all-gather.3.cloned.1.call-start = ((), (), s32[]{:S(2)}) async-start(), calls=%async_computation.1 | async-start | bytes 8912896 | tf_op jit(solution)/shard_map/all_gather | solution.py:9
  7.9 106.9 %all-gather.5.cloned.1.call-start = ((), (), s32[]{:S(2)}) async-start(), calls=%async_computation.3 | async-start | bytes 2555904 | tf_op jit(solution)/shard_map/all_gather | solution.py:8
  8.6 136.5 %reduce-scatter.2.cloned.1.call-start = ((), (), s32[]{:S(2)}) async-start(), calls=%async_computation.2 | async-start | bytes 2555904 | tf_op jit(solution)/shard_map/reduce_scatter | solution.py:13
Sparse Core Ops, SparseCore 0:
  10.2 75.4 all-gather.2
  87.2 27.5 all-gather.4
  117.6 27.5 reduce-scatter.1
where the time goes:
time: 153 us; the launch traced here: 152 us
  waiting for transfers between devices  94.7 us (62%)
  matrix products  43.2 us (28%)
  between operations  13.7 us (9%)
    all_gather x1, waiting for transfers between devices, local(): grad_all = lax.all_gather(grad_out, 'tensor', axis=0, tiled=True)  77 us
    dot_general x1, matrix products, local(): lax.dot_general(grad_all, down_weight, (((1,), (1,)), ((), ())), preferre...  22.1 us
    dot_general x1, matrix products, local(): lax.dot_general(hidden_all, grad_all, (((0,), (0,)), ((), ())), preferred...  21 us
    reduce_scatter x1, waiting for transfers between devices, local(): lax.psum_scatter(lax.dot_general(grad_all, down_weight, (((1,), (1,)), ((...  9.33 us
    all_gather x1, waiting for transfers between devices, local(): hidden_all = lax.all_gather(hidden, 'dp', axis=0, tiled=True)  6.97 us
  transfers between devices with their start and end apart: 3, of which 3 were waited for; matrix products, arithmetic and copies ran while one was open for 28% of the time, Pallas kernels for 0%

commit v1 on v0

v1 whole, which is shorter than its diff:
```python
import functools

import jax
import jax.numpy as jnp
from jax import lax
from jax.experimental import pallas as pl
from jax.experimental.pallas import tpu as pltpu
from jax.sharding import PartitionSpec as P

MESH = pl.DeviceIdType.MESH
Z = 4
AHEAD = 2


def tiles_of(extent, tile):
    return extent // tile, extent % tile


def gather_kernel(ny, halves, chunks, x_ref, w_ref, *refs):
    n_out = 3 if halves else 2
    g_out, part_outs = refs[0], refs[1:n_out]
    g, w, acc, part, own_sem, w_sem, g_sem, out_sem, send_sem, recv_sem = refs[n_out:]
    rows = x_ref.shape[0]
    width = g.shape[2]
    hidden_units = w.shape[1]

    me = lax.axis_index("tensor")
    core = lax.rem(me, 2)
    y = lax.rem(lax.div(me, 2), ny)
    z = lax.div(me, 2 * ny)

    def place(dz, dy, other_core=False):
        zz = lax.rem(z + dz, Z)
        yy = lax.rem(y + dy, ny)
        cc = 1 - core if other_core else core
        return (zz * ny + yy) * 2 + cc

    def block(c, who):
        return g.at[c, pl.ds(pl.multiple_of(who * rows, rows), rows), :]

    def remote(c, shard, slot, target):
        return pltpu.make_async_remote_copy(
            src_ref=block(c, shard),
            dst_ref=block(c, shard),
            send_sem=send_sem.at[c, slot],
            recv_sem=recv_sem.at[c, shard],
            device_id={"tensor": target},
            device_id_type=MESH,
        )

    def along_z(c, dz):
        return remote(c, me, dz - 1, place(dz, 0))

    def along_y(c, dz, dy):
        return remote(c, place(dz, 0), Z - 1 + dz * (ny - 1) + dy - 1, place(0, dy))

    def to_core(c, dz, dy):
        return remote(c, place(dz, dy), Z - 1 + Z * (ny - 1) + dz * ny + dy, place(0, 0, True))

    def arrived(c, shard):
        remote(c, shard, 0, place(0, 0, True)).wait_recv()

    def own(c):
        columns = pl.ds(pl.multiple_of(c * width, width), width)
        return pltpu.make_async_copy(x_ref.at[:, columns], block(c, me), own_sem.at[c])

    def weights(c):
        columns = pl.ds(pl.multiple_of(c * width, width), width)
        return pltpu.make_async_copy(w_ref.at[:, columns], w.at[c], w_sem.at[c])

    def keep(c):
        return pltpu.make_async_copy(g.at[c], g_out.at[c], g_sem.at[c])

    @pl.loop(0, chunks)
    def _(c):
        own(c).start()

    @pl.loop(0, chunks)
    def _(c):
        weights(c).start()

    barrier = pltpu.get_barrier_semaphore()
    partners = [place(dz, 0) for dz in range(1, Z)] + [place(0, dy) for dy in range(1, ny)] + [place(0, 0, True)]
    for partner in partners:
        pl.semaphore_signal(barrier, inc=1, device_id={"tensor": partner}, device_id_type=MESH)
    pl.semaphore_wait(barrier, len(partners))

    def send_own(c):
        own(c).wait()
        for dz in range(1, Z):
            along_z(c, dz).start()
        for dy in range(1, ny):
            along_y(c, 0, dy).start()
        to_core(c, 0, 0).start()

    def pass_on_z(c):
        for dz in range(1, Z):
            arrived(c, place(dz, 0))
            for dy in range(1, ny):
                along_y(c, dz, dy).start()
            to_core(c, dz, 0).start()

    def pass_on_y(c):
        for dz in range(Z):
            for dy in range(1, ny):
                arrived(c, place(dz, dy))
                to_core(c, dz, dy).start()

    def multiply(c):
        for dz in range(Z):
            for dy in range(ny):
                arrived(c, place(dz, dy, True))
        keep(c).start()
        weights(c).wait()
        full, rest = tiles_of(hidden_units, 256)

        def tile(at, size):
            acc[:, pl.ds(at, size)] += lax.dot_general(
                g[c], w[c, pl.ds(at, size), :], (((1,), (1,)), ((), ())), preferred_element_type=jnp.float32
            )

        @pl.loop(0, full)
        def _(j):
            tile(pl.multiple_of(j * 256, 256), 256)

        if rest:
            tile(full * 256, rest)

    for c in range(min(AHEAD, chunks)):
        send_own(c)
    acc[...] = jnp.zeros_like(acc)

    @pl.loop(0, chunks + 2)
    def _(i):
        @pl.when(i + AHEAD < chunks)
        def _():
            send_own(i + AHEAD)

        @pl.when(i < chunks)
        def _():
            pass_on_z(i)

        @pl.when(jnp.logical_and(i >= 1, i < chunks + 1))
        def _():
            pass_on_y(i - 1)

        @pl.when(i >= 2)
        def _():
            multiply(i - 2)

    @pl.loop(0, part.shape[0] // 64)
    def _(r):
        some = pl.ds(pl.multiple_of(r * 64, 64), 64)
        part[some, :] = acc[some, :].astype(part.dtype)

    if halves:
        half = part.shape[0] // 2
        dp = lax.axis_index("dp")
        outs = [
            pltpu.make_async_copy(
                part.at[pl.ds(pl.multiple_of(which * half, half), half), :], part_outs[n], out_sem.at[n]
            )
            for n, which in enumerate((dp, 1 - dp))
        ]
    else:
        outs = [pltpu.make_async_copy(part, part_outs[0], out_sem.at[0])]
    for out in outs:
        out.start()

    @pl.loop(0, chunks)
    def _(c):
        for dz in range(1, Z):
            along_z(c, dz).wait_send()
        for dz in range(Z):
            for dy in range(1, ny):
                along_y(c, dz, dy).wait_send()
        for dz in range(Z):
            for dy in range(ny):
                to_core(c, dz, dy).wait_send()
        keep(c).wait()

    for out in outs:
        out.wait()


def gather_and_multiply(grad_out, weight, n_dp, n_tensor):
    rows, columns = grad_out.shape
    units = weight.shape[0]
    ny = n_tensor // (2 * Z)
    width = 1024
    chunks = columns // width
    tokens = rows * n_tensor
    halves = n_dp == 2
    sends = Z - 1 + Z * (ny - 1) + Z * ny
    bf16 = jnp.bfloat16
    if halves:
        part_shapes = (jax.ShapeDtypeStruct((tokens // 2, units), bf16),) * 2
    else:
        part_shapes = (jax.ShapeDtypeStruct((tokens, units), bf16),)
    any_space = pl.BlockSpec(memory_space=pl.ANY)
    dma = pltpu.SemaphoreType.DMA
    return pl.pallas_call(
        functools.partial(gather_kernel, ny, halves, chunks),
        out_shape=(jax.ShapeDtypeStruct((chunks, tokens, width), bf16), *part_shapes),
        in_specs=[any_space] * 2,
        out_specs=(any_space,) * (1 + len(part_shapes)),
        scratch_shapes=[
            pltpu.VMEM((chunks, tokens, width), bf16),
            pltpu.VMEM((chunks, units, width), bf16),
            pltpu.VMEM((tokens, units), jnp.float32),
            pltpu.VMEM((tokens, units), bf16),
            dma((chunks,)),
            dma((chunks,)),
            dma((chunks,)),
            dma((2,)),
            dma((chunks, sends)),
            dma((chunks, n_tensor)),
        ],
        compiler_params=pltpu.CompilerParams(
            collective_id=0, has_side_effects=True, vmem_limit_bytes=56 * 1024 * 1024
        ),
        cost_estimate=pl.CostEstimate(
            flops=8 * tokens * units * columns, bytes_accessed=120 * 1024 * 1024, transcendentals=0
        ),
        name="gather_multiply",
    )(grad_out, weight)


def weight_kernel(hidden_ref, g_ref, out_ref, turned):
    @pl.when(pl.program_id(0) == 0)
    def _():
        turned[...] = hidden_ref[...].T

    size = turned.shape[0] // 2 if turned.shape[0] // 2 % 16 == 0 else turned.shape[0]

    @pl.loop(0, turned.shape[0] // size)
    def _(m):
        some = pl.ds(pl.multiple_of(m * size, size), size)
        out_ref[some, :] = jnp.dot(
            turned[some, :], g_ref[...], preferred_element_type=jnp.float32
        ).astype(out_ref.dtype)


def weight_grad_of(hidden_all, g):
    tokens, units = hidden_all.shape
    chunks, _, width = g.shape
    block = 512
    per = width // block
    return pl.pallas_call(
        weight_kernel,
        grid=(chunks * per,),
        out_shape=jax.ShapeDtypeStruct((units, chunks * width), jnp.bfloat16),
        in_specs=[
            pl.BlockSpec((tokens, units), lambda j: (0, 0)),
            pl.BlockSpec((None, tokens, block), lambda j: (j // per, 0, j % per)),
        ],
        out_specs=pl.BlockSpec((units, block), lambda j: (0, j)),
        scratch_shapes=[pltpu.VMEM((units, tokens), jnp.bfloat16)],
        compiler_params=pltpu.CompilerParams(vmem_limit_bytes=56 * 1024 * 1024),
        cost_estimate=pl.CostEstimate(
            flops=2 * tokens * units * chunks * width,
            bytes_accessed=2 * (units + tokens) * chunks * width,
            transcendentals=0,
        ),
        name="weight_grad",
    )(hidden_all, g)


def local(n_dp, n_tensor, grad_out, hidden, down_weight):
    hidden_all = lax.all_gather(hidden, "dp", axis=0, tiled=True)
    g, *parts = gather_and_multiply(grad_out, down_weight, n_dp, n_tensor)
    if n_dp == 2:
        mine, theirs = parts
        got = lax.ppermute(theirs, "dp", [(0, 1), (1, 0)])
        weight_grad = weight_grad_of(hidden_all, g)
        mine, weight_grad = lax.optimization_barrier((mine, weight_grad))
        grad_hidden = (mine.astype(jnp.float32) + got.astype(jnp.float32)).astype(jnp.bfloat16)
    else:
        grad_hidden = lax.psum_scatter(parts[0], "dp", scatter_dimension=0, tiled=True)
        weight_grad = weight_grad_of(hidden_all, g)
    return grad_hidden, weight_grad


def solution(mesh):
    return jax.shard_map(
        functools.partial(local, mesh.shape["dp"], mesh.shape["tensor"]),
        mesh=mesh,
        in_specs=(P("tensor", "dp"), P("dp", "tensor"), P("tensor", "dp")),
        out_specs=(P("dp", "tensor"), P("tensor", "dp")),
        check_vma=False,
    )
```

time: 153 us -> 113 us (0.74)
  Pallas kernels: 0 us -> 95.1 us
  waiting for transfers between devices: 94.7 us -> 0.68 us
  matrix products: 43.2 us -> 0 us
    pallas_call x0 -> x2, Pallas kernels: none -> 95.1 us  [the longest x1 70.3 us: gather_and_multiply(): pl.pallas_call(functools.partial(gather_kernel, ny, halves, chunks), out_...]
    all_gather x1 -> x0, waiting for transfers between devices: 77 us -> none  [local(): grad_all = lax.all_gather(grad_out, 'tensor', axis=0, tiled=True)]
    dot_general x2 -> x0, matrix products: 43.2 us -> none  [the longest x1 22.1 us: local(): lax.dot_general(grad_all, down_weight, (((1,), (1,)), ((), ())), preferre...]
    reduce_scatter x1 -> x0, waiting for transfers between devices: 9.33 us -> none  [local(): lax.psum_scatter(lax.dot_general(grad_all, down_weight, (((1,), (1,)), ((...]
    all_gather x1, waiting for transfers between devices: 6.97 us -> 0.01 us  [local(): hidden_all = lax.all_gather(hidden, 'dp', axis=0, tiled=True)]
    ppermute x0 -> x1, starting transfers between devices: none -> 1.56 us  [local(): got = lax.ppermute(theirs, 'dp', [(0, 1), (1, 0)])]
  transfers between devices with their start and end apart: 3 -> 2, of which waited for: 3 -> 0; matrix products, arithmetic and copies ran while one was open for 28% -> 0% of each run, Pallas kernels for 0% -> 85%
where the time goes in v1:
time: 113 us
  Pallas kernels  95.1 us (84%)
  between operations  14 us (12%)
  starting transfers between devices  1.6 us (1%)
    pallas_call x1, Pallas kernels, gather_and_multiply(): pl.pallas_call(functools.partial(gather_kernel, ny, halves, chunks), out_...  70.3 us
    pallas_call x1, Pallas kernels, weight_grad_of(): pl.pallas_call(weight_kernel, grid=(chunks * per,), out_shape=jax.ShapeDt...  24.8 us
  transfers between devices with their start and end apart: 2, of which 0 were waited for; matrix products, arithmetic and copies ran while one was open for 0% of the time, Pallas kernels for 85%

profile of v1, /device:TPU:8, one launch (start us, length us, event | category | flops | bytes accessed | tf_op | source)
XLA Modules:
  0.0 112.5 jit_solution(5952777704302945906)
XLA Ops:
  7.2 0.0 all-gather.2.cloned.1.call-start
  7.2 0.7 all-gather.2.cloned.1.call-update
  7.9 70.3 %gather_multiply.1 = (bf16[8,512,1024]{2,1,0:T(8,128)(2,1)}, bf16[256,1664]{1,0:T(8,128)(2,1)}, bf16[256,1664]{1,0:T(8,128)(2,1)}) custom-call(bf16[32,8192]{1,0:T(8,128)(2,1)} %x_ref.1, bf16[1664,8192]{1,0:T(8,128)(2,1)} %w_ref.1), custom_call_target="tpu_custom_call" | custom-call | flops 55834574848 | bytes 125829120 | tf_op jit(solution)/shard_map/gather_multiply/pallas_call | solution.py:202
  78.2 1.6 %collective-permute-start = (bf16[256,1664]{1,0:T(8,128)(2,1)}, bf16[256,1664]{1,0:T(8,128)(2,1)S(1)}, u32[]{:S(2)}, u32[]{:S(2)}) collective-permute-start(bf16[256,1664]{1,0:T(8,128)(2,1)} %get-tuple-element.10), channel_id=1, source_target_pairs={{0,16},{16,0},{1,17},{17,1},{2,18},{18,2},{3,19},{19,3},{4,20},{20... | collective-permute-start | bytes 2555912 | tf_op jit(solution)/shard_map/ppermute | solution.py:274
  79.8 0.0 all-gather.2.cloned.1.call-done.hidden_ref
  79.8 0.0 copy-start
  79.8 24.8 %weight_grad.1 = bf16[1664,8192]{1,0:T(8,128)(2,1)} custom-call(bf16[512,1664]{1,0:T(8,128)(2,1)} %all-gather.2.cloned.1.call-done.hidden_ref, bf16[8,512,1024]{2,1,0:T(8,128)(2,1)} %get-tuple-element.8.g_ref), custom_call_target="tpu_custom_call" | custom-call | flops 13958643712 | bytes 35651584 | tf_op jit(solution)/shard_map/weight_grad/pallas_call | solution.py:249
  104.6 0.0 collective-permute-done
  104.6 0.0 copy-done
  104.6 1.1 add_convert_fusion
Async XLA Ops:
  7.2 72.6 %all-gather.2.cloned.1.call-start = ((), (), s32[]{:S(2)}) async-start(), calls=%async_computation | async-start | bytes 2555904 | tf_op jit(solution)/shard_map/all_gather | solution.py:270
  78.2 26.4 %collective-permute-start = (bf16[256,1664]{1,0:T(8,128)(2,1)}, bf16[256,1664]{1,0:T(8,128)(2,1)S(1)}, u32[]{:S(2)}, u32[]{:S(2)}) collective-permute-start(bf16[256,1664]{1,0:T(8,128)(2,1)} %get-tuple-element.10), channel_id=1, source_target_pairs={{0,16},{16,0},{1,17},{17,1},{2,18},{18,2},{3,19},{19,3},{4,20},{20... | collective-permute-start | bytes 2555912 | tf_op jit(solution)/shard_map/ppermute | solution.py:274
  79.8 24.8 %copy-start = (bf16[256,1664]{1,0:T(8,128)(2,1)S(1)}, bf16[256,1664]{1,0:T(8,128)(2,1)}, u32[]{:S(2)}) copy-start(bf16[256,1664]{1,0:T(8,128)(2,1)} %get-tuple-element.9) | copy-start | bytes 2555908
Sparse Core Ops, SparseCore 0:
  9.5 29.8 all-gather.1
